TPU v7x, 256 devices: a whole 4x4x8 slice. The times are simulated.
256 devices in a mesh: grp: 4 (over y_hi, core), idx: 64 (over x, z, y_lo).
Axes of the slice: x: 4, y: 4 (y_hi: 2, y_lo: 2; y = y_hi * 2 + y_lo), z: 8, core: 2. Of those that a mesh axis runs over, the one named last changes fastest.
Arguments:
- queries: bfloat16 [4096, 1024], P(('grp', 'idx')), may hold values from -14 to 14
- exemplars: bfloat16 [262144, 1024], P('idx'), may hold values from -4 to 4
- labels: int32 [262144, 64], P('idx'), may hold values 0 or 1
Outputs:
- risk: float32 [4096, 64], P(('grp', 'idx'))
- density: float32 [4096], P(('grp', 'idx'))
All inputs are finite; a program needn't handle non-finite values. No bound on the sum of `labels` on one device may be relied on, other than what follows from the above.
Results may differ from a plain program's by a relative error of at most 0.004.
Values may be sent and summed in bfloat16 or wider, within the bound.
A program may use at most 128 MiB of HBM per device.

v0:
```python
import math

import jax
import jax.numpy as jnp
from jax import lax
from jax.sharding import PartitionSpec as P

D = 1024


def merged(part, axis, combine):
    gathered = jax.tree.map(lambda a: lax.all_gather(a, axis), part)

    def take(source):
        return jax.tree.map(lambda a: lax.dynamic_index_in_dim(a, source, 0, False), gathered)

    return lax.fori_loop(
        1, lax.axis_size(axis), lambda source, state: combine(state, take(source)), take(0)
    )


def join_lse(left_part, right_part):
    peak = jnp.maximum(left_part[0], right_part[0])
    total = left_part[1] * jnp.exp(left_part[0] - peak) + right_part[1] * jnp.exp(
        right_part[0] - peak
    )
    return (peak, total)


def join_risk(left_part, right_part):
    peak = jnp.maximum(left_part[0], right_part[0])
    left_factor = jnp.exp(left_part[0] - peak)
    right_factor = jnp.exp(right_part[0] - peak)
    total = left_part[1] * left_factor + right_part[1] * right_factor
    numerator = left_part[2] * left_factor[:, None] + right_part[2] * right_factor[:, None]
    return (peak, total, numerator)


def per_device(queries, exemplars, labels):
    score_gain = 3.0 / math.sqrt(D)
    local_rows = queries.shape[0]
    group_rows = local_rows * lax.axis_size("idx")
    total_q = group_rows * lax.axis_size("grp")
    total_e = exemplars.shape[0] * lax.axis_size("idx")
    gathered = lax.all_gather(queries, "idx", axis=0, tiled=True)
    scores = (
        lax.dot_general(
            gathered, exemplars, (((1,), (1,)), ((), ())), preferred_element_type=jnp.float32
        )
        * score_gain
    )
    row_max = jnp.max(scores, axis=1)
    row_sum = jnp.sum(jnp.exp(scores - row_max[:, None]), axis=1)
    col_max = jnp.max(scores, axis=0)
    col_sum = jnp.sum(jnp.exp(scores - col_max[None, :]), axis=0)
    row_max, row_sum = merged((row_max, row_sum), "idx", join_lse)
    col_max, col_sum = merged((col_max, col_sum), "grp", join_lse)
    hub = col_max + jnp.log(col_sum) - math.log(total_q)
    corrected = 2.0 * scores - hub[None, :]
    row_top = jnp.max(corrected, axis=1)
    weights = jnp.exp(corrected - row_top[:, None])
    weight_mass = jnp.sum(weights, axis=1)
    numerator = jnp.dot(
        weights.astype(jnp.bfloat16),
        labels.astype(jnp.bfloat16),
        preferred_element_type=jnp.float32,
    )
    own_start = lax.axis_index("idx") * local_rows
    row_top, weight_mass, numerator = merged((row_top, weight_mass, numerator), "idx", join_risk)
    own_mass = lax.dynamic_slice_in_dim(weight_mass, own_start, local_rows, 0)
    own_numer = lax.dynamic_slice_in_dim(numerator, own_start, local_rows, 0)
    risk_rows = own_numer / own_mass[:, None]
    own_max = lax.dynamic_slice_in_dim(row_max, own_start, local_rows, 0)
    own_sum = lax.dynamic_slice_in_dim(row_sum, own_start, local_rows, 0)
    density = own_max + jnp.log(own_sum) - math.log(total_e)
    return (risk_rows, density)


def solution(mesh):
    in_specs = (P(("grp", "idx"), None), P("idx", None), P("idx", None))
    out_specs = (P(("grp", "idx"), None), P(("grp", "idx")))
    return jax.shard_map(
        per_device, mesh=mesh, in_specs=in_specs, out_specs=out_specs, check_vma=False
    )
```

profile of v0, /device:TPU:8, one launch (start us, length us, event | category | flops | bytes accessed | tf_op | source)
XLA Modules:
  0.0 1127.5 jit_solution(1147884835556906224)
XLA Ops:
  7.9 303.3 %all-gather.10.cloned.1.call-done = bf16[1024,1024]{1,0:T(8,128)(2,1)} async-done(((bf16[16,1024]{1,0:T(8,128)(2,1)}), bf16[1024,1024]{1,0:T(8,128)(2,1)}) %all-gather.10.cloned.1.call-update) | async-done | bytes 2097168 | tf_op jit(solution)/shard_map/all_gather | solution.py:45
  311.2 16.1 %multiply_reduce_fusion = (f32[1024]{0:T(1024)S(1)}, f32[4096]{0:T(1024)S(1)}, f32[1024,4096]{1,0:T(8,128)}) fusion(bf16[1024,1024]{1,0:T(8,128)(2,1)} %all-gather.10.cloned.1.call-done, bf16[4096,1024]{1,0:T(8,128)(2,1)} %param.10), kind=kOutput, calls=%fused_computation.18 | convolution fusion | flops 8602512384 | bytes 27283456 | tf_op jit(solution)/shard_map/dot_general | solution.py:47
  327.3 6.7 all-gather
  334.1 9.7 exponential_reduce_fusion
  343.8 6.8 all-gather.1
  350.8 7.6 fusion.1
  358.4 8.4 fusion.4
  366.8 155.8 %all-gather.2 = f32[65536]{0:T(1024)S(1)} all-gather(f32[1024]{0:T(1024)S(1)} %fusion.1), channel_id=4, replica_groups=mesh['grp'=4,'idx'=64] {'idx'}, dimensions={0}, use_global_device_ids=true | all-gather | bytes 266240 | tf_op jit(solution)/shard_map/all_gather | solution.py:12
  522.6 8.0 fusion.3
  530.6 156.5 %all-gather.3 = f32[65536]{0:T(1024)S(1)} all-gather(f32[1024]{0:T(1024)S(1)} %fusion.3), channel_id=5, replica_groups=mesh['grp'=4,'idx'=64] {'idx'}, dimensions={0}, use_global_device_ids=true | all-gather | bytes 266240 | tf_op jit(solution)/shard_map/all_gather | solution.py:12
  687.2 151.6 %all-gather.6 = f32[65536]{0:T(1024)S(1)} all-gather(f32[1024]{0:T(1024)S(1)} %get-tuple-element.465), channel_id=8, replica_groups=mesh['grp'=4,'idx'=64] {'idx'}, dimensions={0}, use_global_device_ids=true | all-gather | bytes 266240 | tf_op jit(solution)/shard_map/all_gather | solution.py:12
  838.8 154.1 %all-gather.5 = f32[65536]{0:T(1024)S(1)} all-gather(f32[1024]{0:T(1024)S(1)} %get-tuple-element.467), channel_id=7, replica_groups=mesh['grp'=4,'idx'=64] {'idx'}, dimensions={0}, use_global_device_ids=true | all-gather | bytes 266240 | tf_op jit(solution)/shard_map/all_gather | solution.py:12
  993.0 3.7 while.55
  998.5 22.9 %copy.9 = f32[65536,64]{1,0:T(8,128)} copy(f32[65536,64]{0,1:T(8,128)} %all-gather.12.cloned.1.call-done) | data formatting | bytes 33554432 | tf_op jit(solution)/shard_map/while | solution.py:17
  1021.4 98.5 %while.54 = (s32[]{:T(128)}, f32[1024]{0:T(1024)S(1)}, f32[1024]{0:T(1024)S(1)}, f32[1024,64]{1,0:T(8,128)S(1)}, f32[64,1024]{1,0:T(8,128)S(1)}, /*index=5*/f32[...) while((s32[]{:T(128)}, f32[1024]{0:T(1024)S(1)}, f32[1024]{0:T(1024)S(1)}, ...), condition=%wide.region_7.8_spmd, body=%wide.region_6.7_spmd.sunk | while | flops 202757 | bytes 843919 | solution.py:17
  1021.4 1.5 fusion.11
  1023.0 1.5 fusion.11
  1024.6 1.5 fusion.11
  1026.1 1.5 fusion.11
  1027.7 1.5 fusion.11
  1029.2 1.5 fusion.11
  1030.8 1.5 fusion.11
  1032.4 1.5 fusion.11
  1033.9 1.5 fusion.11
  (338 shorter events, 88.3 us)
Async XLA Ops:
  7.2 304.0 %all-gather.10.cloned.1.call-start = ((), (), s32[]{:S(2)}) async-start(), calls=%async_computation | async-start | bytes 2129920 | tf_op jit(solution)/shard_map/all_gather | solution.py:45
  7.9 989.4 %all-gather.12.cloned.1.call-start = ((), (), s32[]{:S(2)}) async-start(), calls=%async_computation.1 | async-start | bytes 17039360 | tf_op jit(solution)/shard_map/all_gather | solution.py:12
  334.1 24.3 %copy-start = (s32[4096,64]{0,1:T(8,128)S(1)}, s32[4096,64]{0,1:T(8,128)}, u32[]{:S(2)}) copy-start(s32[4096,64]{0,1:T(8,128)} %param.11) | copy-start | bytes 3145732
Sparse Core Ops, SparseCore 0:
  9.8 301.3 all-gather.9
  366.9 383.6 all-gather.11
where the time goes:
time: 1130 us
  blocking collectives  632 us (56%)
  waiting for transfers between devices  304 us (27%)
  other arithmetic  123 us (11%)
  local copies, waits for them, and re-layouts  26.3 us (2%)
  matrix products  24.5 us (2%)
  between operations  14.1 us (1%)
    all_gather x6, blocking collectives, merged(): gathered = jax.tree.map(lambda a: lax.all_gather(a, axis), part)  632 us
    all_gather x1, waiting for transfers between devices, per_device(): gathered = lax.all_gather(queries, 'idx', axis=0, tiled=True)  303 us
    add x63, other arithmetic, join_risk(): left_part[2] * left_factor[:, None] + right_part[2] * right_factor[:, None]  94.5 us
    while x2, local copies, waits for them, and re-layouts, merged(): lax.fori_loop(1, lax.axis_size(axis), lambda source, state: combine(state...  23.1 us
  transfers between devices with their start and end apart: 2, of which 1 were waited for; matrix products, arithmetic and copies ran while one was open for 1% of the time, Pallas kernels for 0%

commit v1 on v0

v1 whole, which is shorter than its diff:
```python
import functools
import math

import jax
import jax.numpy as jnp
from jax import lax
from jax.experimental import pallas as pl
from jax.experimental.pallas import tpu as pltpu
from jax.sharding import PartitionSpec as P

X, Z, Y, GROUPS = 4, 8, 2, 4
SHARD = 16
X_ORDER = (0, 1, -1, 2)
Z_ORDER = (0, 1, -1, 2, -2, 3, -3, 4)
FIRST_BASE = {0: 0, 1: 64, -1: 128, 2: 576, -2: 640, 3: 832, -3: 896, 4: 960}
SECOND_BASE = {0: 192, 1: 320, -1: 448, 2: 704}
PIECES = ((0, 1), (1, 2), (3, 2), (5, 2), (7, 1))
BLOCK = 256
WIDE = 1024
CATEGORIES = 64
MASS, TOP, DENS = 64, 65, 66
PACKED = 72
LOG2E = 1.4426950408889634
LOWEST = -1e30
MESH = pl.DeviceIdType.MESH


def row_of(side, dx, dz):
    if side == 0:
        return FIRST_BASE[dz] + SHARD * X_ORDER.index(dx)
    return SECOND_BASE[dx] + SHARD * Z_ORDER.index(dz)


def gather_moves():
    moves = {}
    moves["x+"] = (row_of(0, 0, 0), 1, row_of(0, -1, 0), "xp")
    moves["x-"] = (row_of(0, 0, 0), 1, row_of(0, 1, 0), "xm")
    moves["x2"] = (row_of(0, -1, 0), 1, row_of(0, 2, 0), "xp")
    for k in (1, 2, 3, 4):
        far = 4 if k == 4 else -k
        for half in (0, 1):
            off = 32 * half
            if k < 4 or half == 0:
                moves["z+", k, half] = (FIRST_BASE[1 - k] + off, 2, FIRST_BASE[far] + off, "zp")
            if k < 4 or half == 1:
                moves["z-", k, half] = (FIRST_BASE[k - 1] + off, 2, FIRST_BASE[k] + off, "zm")
        moves["w+", k] = (row_of(1, 0, 1 - k), 1, row_of(1, 0, far), "zp")
        if k < 4:
            moves["w-", k] = (row_of(1, 0, k - 1), 1, row_of(1, 0, k), "zm")
    for g, (start, count) in enumerate(PIECES):
        off = SHARD * start
        moves["v+", g] = (SECOND_BASE[0] + off, count, SECOND_BASE[-1] + off, "xp")
        moves["v-", g] = (SECOND_BASE[0] + off, count, SECOND_BASE[1] + off, "xm")
        if g in (0, 1, 4):
            moves["u+", g] = (SECOND_BASE[-1] + off, count, SECOND_BASE[2] + off, "xp")
        else:
            moves["u-", g] = (SECOND_BASE[1] + off, count, SECOND_BASE[2] + off, "xm")
    return moves


MOVES = gather_moves()
MOVE_IDS = {name: 1 + i for i, name in enumerate(MOVES)}
N_MOVES = 1 + len(MOVES)


def dot_t(a, b):
    return lax.dot_general(a, b, (((1,), (1,)), ((), ())), preferred_element_type=jnp.float32)


def kernel(
    groups, total_q, total_e,
    q_ref, ex_hbm, labels_hbm, risk_ref, density_ref,
    rows, ex, labels_raw, labels, s0, s1, s2, s3,
    top_part0, top_part1, row_top, row_sum, peak0, peak1, col_max, col_sum,
    hubs, hub_row, numer, packed, arrived, spread, last,
    load_sem, send, recv, hub_send, hub_recv, a_send, a_recv, b_send, b_recv,
):
    scores = (s0, s1, s2, s3)
    top_part, peak = (top_part0, top_part1), (peak0, peak1)
    depth = q_ref.shape[1]
    gain = 3.0 / math.sqrt(depth) * LOG2E
    local_e = ex.shape[0]
    chunks = local_e // WIDE
    tiles = WIDE // 128
    g = lax.axis_index("grp")
    me = lax.axis_index("idx")
    x, z, y = me // (Z * Y), (me // Y) % Z, me % Y

    def place(dx, dz, y_at):
        return (g, lax.rem(x + dx + X, X) * (Z * Y) + lax.rem(z + dz + Z, Z) * Y + y_at)

    near = {
        "xp": place(1, 0, y), "xm": place(-1, 0, y), "zp": place(0, 1, y), "zm": place(0, -1, y),
    }
    partner = place(0, 0, 1 - y)
    peers = [(lax.rem(g + k, groups), me) for k in range(1, groups)]

    loads = [
        pltpu.make_async_copy(
            ex_hbm.at[pl.ds(n * WIDE, WIDE)], ex.at[pl.ds(n * WIDE, WIDE)], load_sem.at[n]
        )
        for n in range(chunks)
    ]
    label_load = pltpu.make_async_copy(labels_hbm, labels_raw, load_sem.at[chunks])
    label_load.start()
    for load in loads:
        load.start()

    barrier = pltpu.get_barrier_semaphore()
    greeted = [partner, *peers]
    greeted += [place(dx, 0, side) for dx in X_ORDER[1:] for side in (0, 1)]
    greeted += [place(0, dz, y) for dz in Z_ORDER[1:]]
    for other in greeted:
        pl.semaphore_signal(barrier, inc=1, device_id=other, device_id_type=MESH)
    pl.semaphore_wait(barrier, len(greeted))

    def move(name):
        source, count, target, way = MOVES[name]
        sem = MOVE_IDS[name]
        return pltpu.make_async_remote_copy(
            src_ref=rows.at[pl.ds(source, count * SHARD)],
            dst_ref=rows.at[pl.ds(target, count * SHARD)],
            send_sem=send.at[sem], recv_sem=recv.at[sem],
            device_id=near[way], device_id_type=MESH,
        )

    def go(*names):
        for name in names:
            move(name).start()

    def got(*names):
        for name in names:
            move(name).wait_recv()

    def cross(at):
        return pltpu.make_async_remote_copy(
            src_ref=q_ref, dst_ref=rows.at[pl.ds(pl.multiple_of(at, SHARD), SHARD)],
            send_sem=send.at[0], recv_sem=recv.at[0], device_id=partner, device_id_type=MESH,
        )

    own_row = y * row_of(1, 0, 0)
    cross(own_row).start()
    rows[pl.ds(pl.multiple_of(own_row, SHARD), SHARD), :] = q_ref[...]

    label_load.wait()
    rest = lax.broadcasted_iota(jnp.int32, (128 - CATEGORIES, WIDE), 0) + CATEGORIES
    for n in range(chunks):
        at = pl.ds(n * WIDE, WIDE)
        labels[0:CATEGORIES, at] = labels_raw[:, at].astype(jnp.float32).astype(jnp.bfloat16)
        labels[CATEGORIES:128, at] = jnp.where(rest == MASS, 1.0, 0.0).astype(jnp.bfloat16)
    row_sum[...] = jnp.zeros_like(row_sum)
    col_max[...] = jnp.full_like(col_max, LOWEST)
    col_sum[...] = jnp.zeros_like(col_sum)

    cross((1 - y) * row_of(1, 0, 0)).wait_recv()
    go("x+", "x-", ("w+", 1), ("w-", 1), ("v+", 0), ("v-", 0))
    got("x+", "x-")
    go("x2", ("z+", 1, 0), ("z-", 1, 0))
    got(("w+", 1), ("w-", 1))
    go(("w+", 2), ("w-", 2), ("v+", 1), ("v-", 1))
    got("x2")
    go(("z+", 1, 1), ("z-", 1, 1))
    got(("w+", 2), ("w-", 2))
    go(("w+", 3), ("w-", 3), ("v+", 2), ("v-", 2))
    got(("z+", 1, 0), ("z-", 1, 0))
    go(("z+", 2, 0), ("z-", 2, 0))
    got(("w+", 3), ("w-", 3))
    go(("w+", 4), ("v+", 3), ("v-", 3))
    got(("z+", 1, 1), ("z-", 1, 1))
    go(("z+", 2, 1), ("z-", 2, 1))

    def event(at):
        if at == (0, 1):
            got(("w+", 4))
            go(("v+", 4), ("v-", 4))
            got(("v+", 0), ("v-", 0), ("v+", 1), ("v-", 1))
            go(("u+", 0), ("u+", 1))
        if at == (0, 2):
            got(("v+", 2), ("v-", 2))
            go(("u-", 2))
            got(("z+", 2, 0), ("z-", 2, 0))
            go(("z+", 3, 0), ("z-", 3, 0))
        if at == (0, 3):
            got(("v+", 3), ("v-", 3))
            go(("u-", 3))
        if at == (1, 0):
            got(("z+", 2, 1), ("z-", 2, 1))
            go(("z+", 3, 1), ("z-", 3, 1))
            got(("v+", 4), ("v-", 4))
            go(("u+", 4))
        if at == (1, 2):
            got(("z+", 3, 0), ("z-", 3, 0))
            go(("z+", 4, 0))
        if at == (2, 0):
            got(("u+", 0), ("u+", 1), ("u-", 2))
            got(("z+", 3, 1), ("z-", 3, 1))
            go(("z-", 4, 1))
        if at == (3, 0):
            got(("u-", 3), ("u+", 4), ("z+", 4, 0), ("z-", 4, 1))

    def score(b, n):
        at = pl.ds(n * WIDE, WIDE)
        s = dot_t(rows[pl.ds(b * BLOCK, BLOCK), :], ex[at, :]) * gain
        scores[b][:, at] = s
        top = s[:, 0:128]
        for t in range(1, tiles):
            top = jnp.maximum(top, s[:, t * 128 : (t + 1) * 128])
        ref = top_part[b % 2]
        ref[...] = top if n == 0 else jnp.maximum(ref[...], top)
        peak[b % 2][:, at] = jnp.max(s.reshape(BLOCK // 8, 8, WIDE), axis=0)

    def total(b, n, tall=32, wide=512):
        at = pl.ds(n * WIDE, WIDE)
        old = col_max[:, at]
        new = jnp.maximum(old, peak[b % 2][:, at])
        col_max[:, at] = new
        scaled = col_sum[:, at] * jnp.exp2(old - new)
        for c in range(0, WIDE, wide):
            shift = new[:, c : c + wide]
            col = scaled[:, c : c + wide]
            for r in range(0, BLOCK, tall):
                s = scores[b][r : r + tall, n * WIDE + c : n * WIDE + c + wide]
                col = col + jnp.exp2(s.reshape(tall // 8, 8, wide) - shift[None]).sum(0)
                mine = pl.ds(b * BLOCK + r, tall)
                top = row_top[mine, :]
                row = row_sum[mine, :]
                for u in range(0, wide, 128):
                    row = row + jnp.exp2(s[:, u : u + 128] - top)
                row_sum[mine, :] = row
            col_sum[:, n * WIDE + c : n * WIDE + c + wide] = col

    def hub_move(k, n):
        at = pl.ds(n * tiles, tiles)
        return pltpu.make_async_remote_copy(
            src_ref=hubs.at[0, at], dst_ref=hubs.at[k, at],
            send_sem=hub_send.at[k, n], recv_sem=hub_recv.at[k, n],
            device_id=peers[k - 1], device_id_type=MESH,
        )

    def hub_part(n):
        at = pl.ds(n * WIDE, WIDE)
        top = jnp.max(col_max[:, at], axis=0, keepdims=True)
        whole = jnp.sum(col_sum[:, at] * jnp.exp2(col_max[:, at] - top), axis=0, keepdims=True)
        lse = top + jnp.log(whole) * LOG2E
        for t in range(tiles):
            hubs[0, n * tiles + t : n * tiles + t + 1, :] = lse[:, t * 128 : (t + 1) * 128]
        for k in range(1, groups):
            hub_move(k, n).start()

    blocks = len(scores)
    for b in range(blocks + 1):
        for n in range(chunks):
            event((b, n))
            if b < blocks:
                if b == 0:
                    loads[n].wait()
                score(b, n)
            if b > 0:
                total(b - 1, n)
            if b == blocks:
                hub_part(n)
        if b < blocks:
            row_top[pl.ds(b * BLOCK, BLOCK), :] = jnp.broadcast_to(
                jnp.max(top_part[b % 2][...], axis=1, keepdims=True), (BLOCK, 128)
            )

    for k in range(1, groups):
        for n in range(chunks):
            hub_move(k, n).wait_recv()
    parts = [hubs[k] for k in range(groups)]
    top = functools.reduce(jnp.maximum, parts)
    whole = sum(jnp.exp2(part - top) for part in parts)
    half_hub = 0.5 * (top + jnp.log(whole) * LOG2E - math.log2(total_q))
    for t in range(local_e // 128):
        hub_row[:, t * 128 : (t + 1) * 128] = half_hub[t : t + 1, :]

    wide_lane = lax.broadcasted_iota(jnp.int32, (BLOCK, 128), 1)
    half = local_e // 2

    def weigh(b):
        ref = scores[b]
        best = jnp.full((BLOCK, 128), LOWEST, jnp.float32)
        for t in range(local_e // 128):
            at = slice(t * 128, (t + 1) * 128)
            best = jnp.maximum(best, ref[:, at] - hub_row[0:1, at])
        top = jnp.max(best, axis=1, keepdims=True)
        acc = jnp.zeros((BLOCK, 128), jnp.float32)
        for c in range(0, local_e, half):
            at = slice(c, c + half)
            over = ref[:, at] - hub_row[0:1, at] - top
            weights = jnp.exp2(over + over).astype(jnp.bfloat16)
            acc = acc + dot_t(weights, labels[:, at])
        mine = pl.ds(b * BLOCK, BLOCK)
        dens = row_top[mine, :] + LOG2E * jnp.log(
            jnp.sum(row_sum[mine, :], axis=1, keepdims=True)
        )
        numer[mine, :] = jnp.where(
            wide_lane == TOP, top, jnp.where(wide_lane == DENS, dens, acc)
        )

    def pack(side, dx):
        if side == 1:
            part = numer[SECOND_BASE[dx] : SECOND_BASE[dx] + 128, :]
        else:
            starts = [row_of(0, dx, dz) for dz in Z_ORDER]
            part = jnp.concatenate([numer[r : r + SHARD, :] for r in starts], axis=0)
        packed[2 * X_ORDER.index(dx) + side] = part.T[0:PACKED, :]

    def a_move(slot, to):
        return pltpu.make_async_remote_copy(
            src_ref=packed.at[slot], dst_ref=arrived.at[slot - slot % 2 + y],
            send_sem=a_send.at[slot], recv_sem=a_recv.at[slot - slot % 2 + y],
            device_id=to, device_id_type=MESH,
        )

    def a_wait(slot):
        pltpu.make_async_remote_copy(
            src_ref=arrived.at[slot], dst_ref=arrived.at[slot],
            send_sem=a_send.at[slot], recv_sem=a_recv.at[slot],
            device_id=partner, device_id_type=MESH,
        ).wait_recv()

    def deliver(dx, side):
        pack(side, dx)
        slot = 2 * X_ORDER.index(dx) + side
        a_move(slot, place(dx, 0, side)).start()

    weigh(0)
    weigh(1)
    pack(1, 0)
    deliver(1, 1)
    weigh(2)
    deliver(-1, 1)
    weigh(3)
    deliver(2, 1)
    for dx in (2, 1, -1):
        deliver(dx, 0)
    pack(0, 0)
    a_move(1 - y, partner).start()
    arrived[y] = packed[y]

    a_wait(1 - y)
    for slot in range(2, 2 * X):
        a_wait(slot)
    parts = [arrived[k] for k in range(2 * X)]
    tops = [part[TOP : TOP + 1, :] for part in parts]
    dens = [part[DENS : DENS + 1, :] for part in parts]
    top = functools.reduce(jnp.maximum, tops)
    summed = jnp.zeros((PACKED, 128), jnp.float32)
    for part, mine in zip(parts, tops):
        over = mine - top
        summed = summed + part * jnp.exp2(over + over)
    dens_top = functools.reduce(jnp.maximum, dens)
    dens_sum = sum(jnp.exp2(mine - dens_top) for mine in dens)
    dens_lse = dens_top + jnp.log(dens_sum) * LOG2E
    place_row = lax.broadcasted_iota(jnp.int32, (PACKED, 128), 0)
    summed = jnp.where(place_row == TOP, top, jnp.where(place_row == DENS, dens_lse, summed))
    full = jnp.concatenate([summed, jnp.zeros((128 - PACKED, 128), jnp.float32)], axis=0)
    spread[...] = full.T

    def b_move(k):
        return pltpu.make_async_remote_copy(
            src_ref=spread.at[pl.ds(k * SHARD, SHARD)], dst_ref=last.at[k],
            send_sem=b_send.at[k], recv_sem=b_recv.at[k],
            device_id=place(0, Z_ORDER[k], y), device_id_type=MESH,
        )

    for k in (7, 6, 5, 4, 3, 2, 1):
        b_move(k).start()
    last[0] = spread[0:SHARD, :]
    for k in range(1, Z):
        b_move(k).wait_recv()
    parts = [last[k] for k in range(Z)]
    tops = [part[:, TOP : TOP + 1] for part in parts]
    dens = [part[:, DENS : DENS + 1] for part in parts]
    top = functools.reduce(jnp.maximum, tops)
    summed = jnp.zeros((SHARD, 128), jnp.float32)
    for part, mine in zip(parts, tops):
        over = mine - top
        summed = summed + part * jnp.exp2(over + over)
    risk_ref[...] = summed[:, 0:CATEGORIES] / summed[:, MASS : MASS + 1]
    dens_top = functools.reduce(jnp.maximum, dens)
    dens_sum = sum(jnp.exp2(mine - dens_top) for mine in dens)
    density = dens_top / LOG2E + jnp.log(dens_sum) - math.log(total_e)
    density_ref[...] = jnp.broadcast_to(density, (SHARD, 128)).T[0:1, 0:SHARD]

    cross(own_row).wait_send()
    for name in MOVES:
        move(name).wait_send()
    for k in range(1, groups):
        for n in range(chunks):
            hub_move(k, n).wait_send()
    for slot in range(2, 2 * X):
        a_move(slot, partner).wait_send()
    a_move(1 - y, partner).wait_send()
    for k in range(1, Z):
        b_move(k).wait_send()


def per_device(queries, exemplars, labels):
    groups = lax.axis_size("grp")
    devices = lax.axis_size("idx")
    local_q, depth = queries.shape
    local_e = exemplars.shape[0]
    group_q = local_q * devices
    f32, bf16 = jnp.float32, jnp.bfloat16
    vmem, dma = pltpu.VMEM, pltpu.SemaphoreType.DMA
    chunks = local_e // WIDE
    here = pl.BlockSpec(memory_space=pltpu.VMEM)
    away = pl.BlockSpec(memory_space=pl.ANY)
    risk, density = pl.pallas_call(
        functools.partial(kernel, groups, group_q * groups, local_e * devices),
        out_shape=(
            jax.ShapeDtypeStruct((local_q, CATEGORIES), f32),
            jax.ShapeDtypeStruct((1, local_q), f32),
        ),
        in_specs=[here, away, away],
        out_specs=(here, here),
        scratch_shapes=[
            vmem((group_q, depth), bf16),
            vmem((local_e, depth), bf16),
            vmem((CATEGORIES, local_e), jnp.int32),
            vmem((128, local_e), bf16),
            *[vmem((BLOCK, local_e), f32)] * 4,
            *[vmem((BLOCK, 128), f32)] * 2,
            *[vmem((group_q, 128), f32)] * 2,
            *[vmem((8, local_e), f32)] * 4,
            vmem((groups, local_e // 128, 128), f32),
            vmem((1, local_e), f32),
            vmem((group_q, 128), f32),
            vmem((2 * X, PACKED, 128), f32),
            vmem((2 * X, PACKED, 128), f32),
            vmem((128, 128), f32),
            vmem((Z, SHARD, 128), f32),
            dma((chunks + 1,)),
            dma((N_MOVES,)),
            dma((N_MOVES,)),
            dma((groups, chunks)),
            dma((groups, chunks)),
            dma((2 * X,)),
            dma((2 * X,)),
            dma((Z,)),
            dma((Z,)),
        ],
        compiler_params=pltpu.CompilerParams(
            collective_id=0, has_side_effects=True, vmem_limit_bytes=58 * 2**20
        ),
        cost_estimate=pl.CostEstimate(
            flops=2 * group_q * local_e * (depth + 128),
            bytes_accessed=local_e * depth * 2 + local_e * CATEGORIES * 4,
            transcendentals=3 * group_q * local_e,
        ),
        name="prefilter",
    )(queries, exemplars, labels.T)
    return risk, density.reshape(local_q)


def solution(mesh):
    in_specs = (P(("grp", "idx"), None), P("idx", None), P("idx", None))
    out_specs = (P(("grp", "idx"), None), P(("grp", "idx")))
    return jax.shard_map(
        per_device, mesh=mesh, in_specs=in_specs, out_specs=out_specs, check_vma=False
    )
```

time: 1130 us -> 69.5 us (0.06)
  the two profiles are of different devices: /device:TPU:8 before, /device:TPU:1 now
where the time goes in v1:
time: 69.5 us; the launch traced here: 69.3 us
  Pallas kernels  66.2 us (95%)
  local copies, waits for them, and re-layouts  2.43 us (3%)
    pallas_call x1, Pallas kernels, per_device(): pl.pallas_call(functools.partial(kernel, groups, group_q * groups, local_...  66.2 us
    unnamed x2, local copies, waits for them, and re-layouts  2.43 us

profile of v1, /device:TPU:1, one launch (start us, length us, event | category | flops | bytes accessed | tf_op | source)
XLA Modules:
  0.0 69.3 jit_solution(18193919091497646529)
XLA Ops:
  0.6 66.2 %prefilter.1 = (f32[16,64]{1,0:T(8,128)}, f32[1,16]{1,0:T(1,128)}) custom-call(bf16[16,1024]{1,0:T(8,128)(2,1)} %q_ref.1, bf16[4096,1024]{1,0:T(8,128)(2,1)} %ex_hbm.1, s32[64,4096]{1,0:T(8,128)} %bitcast.2), custom_call_target="tpu_custom_call" | custom-call | flops 9663676416 | bytes 9437184 | tf_op jit(solution)/shard_map/prefilter/pallas_call | solution.py:411
  66.8 1.3 %copy.7 = f32[16,64]{1,0:T(8,128)} copy(f32[16,64]{1,0:T(8,128)} %get-tuple-element.8) | data formatting | bytes 8192
  68.1 1.1 %copy.8 = f32[16]{0:T(128)} copy(f32[16]{0:T(128)} %bitcast.3) | data formatting | bytes 128

commit v2 on v1

v2 whole, which is shorter than its diff:
```python
import functools
import math

import jax
import jax.numpy as jnp
from jax import lax
from jax.experimental import pallas as pl
from jax.experimental.pallas import tpu as pltpu
from jax.sharding import PartitionSpec as P

X, Z, Y, GROUPS = 4, 8, 2, 4
SHARD = 16
X_ORDER = (0, 1, -1, 2)
Z_ORDER = (0, 1, -1, 2, -2, 3, -3, 4)
FIRST_BASE = {0: 0, 1: 64, -1: 128, 2: 256, -2: 320, 3: 768, -3: 832, 4: 896}
NEAR_BASE = {0: 192, 1: 384, -1: 448, 2: 704}
FAR_BASE = {0: 512, 1: 576, -1: 640, 2: 960}
PIECES = ((0, 1), (1, 2), (2, 1), (-2, 1), (3, 2), (4, 1))
BLOCK = 256
WIDE = 1024
CATEGORIES = 64
MASS, TOP, DENS, UNUSED = 64, 67, 70, 73
LOG2E = 1.4426950408889634
LOWEST = -1e30
MESH = pl.DeviceIdType.MESH


def row_of(side, dx, dz):
    if side == 0:
        return FIRST_BASE[dz] + SHARD * X_ORDER.index(dx)
    at = Z_ORDER.index(dz)
    return NEAR_BASE[dx] + SHARD * at if at < 4 else FAR_BASE[dx] + SHARD * (at - 4)


def gather_moves():
    moves = {}
    for k in (1, 2, 3, 4):
        far = 4 if k == 4 else -k
        for half in (0, 1):
            off = 32 * half
            if k < 4 or half == 0:
                moves["z+", k, half] = (FIRST_BASE[1 - k] + off, 2, FIRST_BASE[far] + off, "zp")
            if k < 4 or half == 1:
                moves["z-", k, half] = (FIRST_BASE[k - 1] + off, 2, FIRST_BASE[k] + off, "zm")
    for g, (dz, count) in enumerate(PIECES):
        own = row_of(1, 0, dz)
        moves["v+", g] = (own, count, row_of(1, -1, dz), "xp")
        moves["v-", g] = (own, count, row_of(1, 1, dz), "xm")
        if g in (0, 1, 5):
            moves["u+", g] = (row_of(1, -1, dz), count, row_of(1, 2, dz), "xp")
        else:
            moves["u-", g] = (row_of(1, 1, dz), count, row_of(1, 2, dz), "xm")
    moves["w+", 3] = (row_of(1, 0, -2), 1, row_of(1, 0, -3), "zp")
    moves["w-", 3] = (row_of(1, 0, 2), 1, row_of(1, 0, 3), "zm")
    moves["w+", 4] = (row_of(1, 0, -2), 1, row_of(1, 0, 4), "zpp")
    for g, (dz, count) in enumerate(PIECES):
        if g > 0:
            moves["f", g] = (row_of(1, 0, dz), count, row_of(1, 0, dz), "partner")
    return moves


MOVES = gather_moves()
EVERY_MOVES = [name for name in MOVES if name[0][0] in "zvu"]
FOUND_MOVES = [name for name in MOVES if name[0] in ("w+", "w-")]
HANDED_MOVES = [name for name in MOVES if name[0] == "f"]
MOVE_IDS = {name: i for i, name in enumerate(MOVES)}
FIRST_WAY = {(0, dx): len(MOVES) + i for i, dx in enumerate(X_ORDER)}
SECOND_WAY = {dz: len(MOVES) + len(X_ORDER) + i for i, dz in enumerate(Z_ORDER[0:5])}
N_MOVES = len(MOVES) + len(X_ORDER) + 5
SENDERS = X * Z * Y


def dot_t(a, b):
    return lax.dot_general(a, b, (((1,), (1,)), ((), ())), preferred_element_type=jnp.float32)


def kernel(
    groups, total_q, total_e,
    q_ref, ex_hbm, labels_hbm, risk_ref, density_ref,
    rows, ex, labels_raw, labels, s0, s1, s2, s3,
    top_part0, top_part1, row_top, row_sum, peak0, peak1, col_max, col_sum,
    best, hubs, hub_row, numer, arrived,
    load_sem, send, recv, own_send, hub_send, hub_recv, sum_send, sum_recv,
):
    scores = (s0, s1, s2, s3)
    top_part, peak = (top_part0, top_part1), (peak0, peak1)
    depth = q_ref.shape[1]
    gain = 3.0 / math.sqrt(depth) * LOG2E
    local_e = ex.shape[0]
    chunks = local_e // WIDE
    tiles = WIDE // 128
    g = lax.axis_index("grp")
    me = lax.axis_index("idx")
    x, z, y = me // (Z * Y), (me // Y) % Z, me % Y

    def place(dx, dz, y_at):
        return (g, lax.rem(x + dx + X, X) * (Z * Y) + lax.rem(z + dz + Z, Z) * Y + y_at)

    near = {
        "xp": place(1, 0, y), "xm": place(-1, 0, y), "zp": place(0, 1, y), "zm": place(0, -1, y),
        "zpp": place(0, 2, y), "partner": place(0, 0, 1 - y),
    }
    partner = near["partner"]
    peers = [(lax.rem(g + k, groups), me) for k in range(1, groups)]

    loads = [
        pltpu.make_async_copy(
            ex_hbm.at[pl.ds(n * WIDE, WIDE)], ex.at[pl.ds(n * WIDE, WIDE)], load_sem.at[n]
        )
        for n in range(chunks)
    ]
    label_load = pltpu.make_async_copy(labels_hbm, labels_raw, load_sem.at[chunks])
    label_load.start()
    for load in loads:
        load.start()

    barrier = pltpu.get_barrier_semaphore()
    greeted = [partner, *peers]
    greeted += [place(dx, 0, side) for dx in X_ORDER[1:] for side in (0, 1)]
    greeted += [place(0, dz, y) for dz in Z_ORDER[1:5]]
    for other in greeted:
        pl.semaphore_signal(barrier, inc=1, device_id=other, device_id_type=MESH)
    pl.semaphore_wait(barrier, len(greeted))

    def move(name):
        source, count, target, way = MOVES[name]
        sem = MOVE_IDS[name]
        return pltpu.make_async_remote_copy(
            src_ref=rows.at[pl.ds(source, count * SHARD)],
            dst_ref=rows.at[pl.ds(target, count * SHARD)],
            send_sem=send.at[sem], recv_sem=recv.at[sem],
            device_id=near[way], device_id_type=MESH,
        )

    def go(*names):
        for name in names:
            move(name).start()

    def got(*names):
        for name in names:
            move(name).wait_recv()

    def away(k, target, sem, to):
        return pltpu.make_async_remote_copy(
            src_ref=q_ref, dst_ref=rows.at[pl.ds(target, SHARD)],
            send_sem=own_send.at[k], recv_sem=recv.at[sem], device_id=to, device_id_type=MESH,
        )

    first_away = [away(0, row_of(0, 0, 0), FIRST_WAY[0, 0], partner)]
    for dx in X_ORDER[1:]:
        back = dx if dx == 2 else -dx
        for side in (0, 1):
            first_away.append(
                away(
                    len(first_away), row_of(0, back, 0), FIRST_WAY[0, back], place(dx, 0, side)
                )
            )
    second_away = [away(0, row_of(1, 0, 0), SECOND_WAY[0], partner)]
    for dz in Z_ORDER[1:5]:
        second_away.append(
            away(len(second_away), row_of(1, 0, -dz), SECOND_WAY[-dz], place(0, dz, y))
        )

    def landed(target, sem):
        away(0, target, sem, partner).wait_recv()

    @pl.when(y == 0)
    def _():
        for copy in first_away:
            copy.start()

    @pl.when(y == 1)
    def _():
        for copy in second_away:
            copy.start()

    own_row = y * row_of(1, 0, 0)
    rows[pl.ds(pl.multiple_of(own_row, SHARD), SHARD), :] = q_ref[...]

    label_load.wait()
    rest = lax.broadcasted_iota(jnp.int32, (128 - CATEGORIES, WIDE), 0) + CATEGORIES
    for n in range(chunks):
        at = pl.ds(n * WIDE, WIDE)
        labels[0:CATEGORIES, at] = labels_raw[:, at].astype(jnp.float32).astype(jnp.bfloat16)
        labels[CATEGORIES:128, at] = jnp.where(rest == MASS, 1.0, 0.0).astype(jnp.bfloat16)
    row_sum[...] = jnp.zeros_like(row_sum)
    col_max[...] = jnp.full_like(col_max, LOWEST)
    col_sum[...] = jnp.zeros_like(col_sum)

    @pl.when(y == 0)
    def _():
        landed(row_of(1, 0, 0), SECOND_WAY[0])

    go(("v+", 0), ("v-", 0))

    @pl.when(y == 1)
    def _():
        landed(row_of(0, 0, 0), FIRST_WAY[0, 0])
        landed(row_of(1, 0, 1), SECOND_WAY[1])
        landed(row_of(1, 0, -1), SECOND_WAY[-1])
        go(("f", 1), ("v+", 1), ("v-", 1))
        landed(row_of(1, 0, 2), SECOND_WAY[2])
        go(("f", 2), ("w-", 3), ("v+", 2), ("v-", 2))
        landed(row_of(1, 0, -2), SECOND_WAY[-2])
        go(("f", 3), ("w+", 3), ("w+", 4), ("v+", 3), ("v-", 3))

    for dx in X_ORDER[1:]:
        landed(row_of(0, dx, 0), FIRST_WAY[0, dx])
    go(("z+", 1, 0), ("z-", 1, 0), ("z+", 1, 1), ("z-", 1, 1))

    @pl.when(y == 0)
    def _():
        for g in (1, 2, 3):
            got(("f", g))
            go(("v+", g), ("v-", g))

    for half in (0, 1):
        got(("z+", 1, half), ("z-", 1, half))
        go(("z+", 2, half), ("z-", 2, half))

    def event(at):
        if at == (0, 1):
            got(("v+", 0), ("v-", 0))
            go(("u+", 0))
        if at == (0, 2):

            @pl.when(y == 1)
            def _():
                got(("w+", 3), ("w-", 3))
                go(("f", 4), ("v+", 4), ("v-", 4))
                got(("w+", 4))
                go(("f", 5), ("v+", 5), ("v-", 5))

        if at == (0, 3):
            got(("v+", 1), ("v-", 1))
            go(("u+", 1))
            got(("v+", 2), ("v-", 2))
            go(("u-", 2))
            got(("v+", 3), ("v-", 3))
            go(("u-", 3))
        if at == (1, 0):
            for half in (0, 1):
                got(("z+", 2, half), ("z-", 2, half))
                go(("z+", 3, half), ("z-", 3, half))
        if at == (1, 1):

            @pl.when(y == 0)
            def _():
                for g in (4, 5):
                    got(("f", g))
                    go(("v+", g), ("v-", g))

        if at == (1, 3):
            got(("z+", 3, 0), ("z-", 3, 0))
            go(("z+", 4, 0))
        if at == (2, 0):
            got(("z+", 3, 1), ("z-", 3, 1))
            go(("z-", 4, 1))
            got(("v+", 4), ("v-", 4))
            go(("u-", 4))
            got(("v+", 5), ("v-", 5))
            go(("u+", 5))
            got(("u+", 0), ("u+", 1), ("u-", 2))
        if at == (3, 0):
            got(("z+", 4, 0), ("z-", 4, 1), ("u-", 3), ("u-", 4), ("u+", 5))

    def score(b, n):
        at = pl.ds(n * WIDE, WIDE)
        s = dot_t(rows[pl.ds(b * BLOCK, BLOCK), :], ex[at, :]) * gain
        scores[b][:, at] = s
        top = s[:, 0:128]
        for t in range(1, tiles):
            top = jnp.maximum(top, s[:, t * 128 : (t + 1) * 128])
        ref = top_part[b % 2]
        ref[...] = top if n == 0 else jnp.maximum(ref[...], top)
        peak[b % 2][:, at] = jnp.max(s.reshape(BLOCK // 8, 8, WIDE), axis=0)

    def total(b, n, rowwise=True, colwise=True, tall=32, wide=512):
        at = pl.ds(n * WIDE, WIDE)
        if colwise:
            old = col_max[:, at]
            new = jnp.maximum(old, peak[b % 2][:, at])
            col_max[:, at] = new
            scaled = col_sum[:, at] * jnp.exp2(old - new)
        for c in range(0, WIDE, wide):
            if colwise:
                shift = new[:, c : c + wide]
                col = scaled[:, c : c + wide]
            for r in range(0, BLOCK, tall):
                s = scores[b][r : r + tall, n * WIDE + c : n * WIDE + c + wide]
                if colwise:
                    col = col + jnp.exp2(s.reshape(tall // 8, 8, wide) - shift[None]).sum(0)
                if rowwise:
                    mine = pl.ds(b * BLOCK + r, tall)
                    top = row_top[mine, :]
                    row = row_sum[mine, :]
                    for u in range(0, wide, 128):
                        row = row + jnp.exp2(s[:, u : u + 128] - top)
                    row_sum[mine, :] = row
            if colwise:
                col_sum[:, n * WIDE + c : n * WIDE + c + wide] = col

    def hub_move(k, n):
        at = pl.ds(n * tiles, tiles)
        return pltpu.make_async_remote_copy(
            src_ref=hubs.at[0, at], dst_ref=hubs.at[k, at],
            send_sem=hub_send.at[k, n], recv_sem=hub_recv.at[k, n],
            device_id=peers[k - 1], device_id_type=MESH,
        )

    def hub_part(n):
        at = pl.ds(n * WIDE, WIDE)
        top = jnp.max(col_max[:, at], axis=0, keepdims=True)
        whole = jnp.sum(col_sum[:, at] * jnp.exp2(col_max[:, at] - top), axis=0, keepdims=True)
        lse = top + jnp.log(whole) * LOG2E
        for t in range(tiles):
            hubs[0, n * tiles + t : n * tiles + t + 1, :] = lse[:, t * 128 : (t + 1) * 128]
        for k in range(1, groups):
            hub_move(k, n).start()

    blocks = len(scores)
    final = blocks - 1
    for b in range(blocks):
        for n in range(chunks):
            event((b, n))
            if b == 0:
                loads[n].wait()
            score(b, n)
            if b > 0:
                total(b - 1, n)
            if b == final:
                total(b, n, rowwise=False)
                hub_part(n)
        row_top[pl.ds(b * BLOCK, BLOCK), :] = jnp.broadcast_to(
            jnp.max(top_part[b % 2][...], axis=1, keepdims=True), (BLOCK, 128)
        )
    for n in range(chunks):
        total(final, n, colwise=False)

    for n in range(chunks):
        at = pl.ds(n * tiles, tiles)
        for k in range(1, groups):
            hub_move(k, n).wait_recv()
        parts = [hubs[k, at] for k in range(groups)]
        top = functools.reduce(jnp.maximum, parts)
        whole = sum(jnp.exp2(part - top) for part in parts)
        half_hub = 0.5 * (top + jnp.log(whole) * LOG2E - math.log2(total_q))
        for t in range(tiles):
            hub_row[:, n * WIDE + t * 128 : n * WIDE + (t + 1) * 128] = half_hub[t : t + 1, :]
        for b in range(blocks):
            mine = pl.ds(b * BLOCK, BLOCK)
            top = scores[b][:, n * WIDE : n * WIDE + 128] - hub_row[:, n * WIDE : n * WIDE + 128]
            for t in range(1, tiles):
                at_t = slice(n * WIDE + t * 128, n * WIDE + (t + 1) * 128)
                top = jnp.maximum(top, scores[b][:, at_t] - hub_row[:, at_t])
            best[mine, :] = top if n == 0 else jnp.maximum(best[mine, :], top)

    wide_lane = lax.broadcasted_iota(jnp.int32, (BLOCK, 128), 1)
    half = local_e // 2

    def weigh(b):
        ref = scores[b]
        mine = pl.ds(b * BLOCK, BLOCK)
        top = jnp.max(best[mine, :], axis=1, keepdims=True)
        acc = jnp.zeros((BLOCK, 128), jnp.float32)
        for c in range(0, local_e, half):
            at = slice(c, c + half)
            over = ref[:, at] - hub_row[0:1, at] - top
            weights = jnp.exp2(over + over).astype(jnp.bfloat16)
            acc = acc + dot_t(weights, labels[:, at])
        dens = row_top[mine, :] + LOG2E * jnp.log(
            jnp.sum(row_sum[mine, :], axis=1, keepdims=True)
        )
        figure = jnp.where(
            wide_lane < TOP, acc[:, MASS : MASS + 1], jnp.where(wide_lane < DENS, top, dens)
        )
        high = figure.astype(jnp.bfloat16).astype(jnp.float32)
        middle = (figure - high).astype(jnp.bfloat16).astype(jnp.float32)
        low = figure - high - middle
        turn = lax.rem(wide_lane - MASS, 3)
        piece = jnp.where(turn == 0, high, jnp.where(turn == 1, middle, low))
        piece = jnp.where(wide_lane < UNUSED, piece, 0.0)
        numer[mine, :] = jnp.where(wide_lane < MASS, acc, piece).astype(jnp.bfloat16)

    def slot_of(side, dx, dz):
        return (side * X + X_ORDER.index(dx)) * Z + Z_ORDER.index(dz)

    def sum_move(source, sender, slot, to):
        return pltpu.make_async_remote_copy(
            src_ref=numer.at[pl.ds(source, SHARD)], dst_ref=arrived.at[slot],
            send_sem=sum_send.at[sender], recv_sem=sum_recv.at[slot],
            device_id=to, device_id_type=MESH,
        )

    others = [
        (side, dx, dz)
        for dz in reversed(Z_ORDER)
        for dx in reversed(X_ORDER)
        for side in (0, 1)
        if (dx, dz) != (0, 0)
    ]

    def hand_out(side, dx, dz):
        return sum_move(
            row_of(side, dx, dz), slot_of(side, dx, dz), slot_of(0, dx, dz) + y * (X * Z),
            place(dx, dz, side),
        )

    partner_row = pl.multiple_of((1 - y) * row_of(1, 0, 0), SHARD)
    hand_partner = sum_move(partner_row, 0, y * (X * Z), partner)
    for b in reversed(range(blocks)):
        weigh(b)
        for where in others:
            if row_of(*where) // BLOCK == b:
                hand_out(*where).start()
    hand_partner.start()
    arrived[y * (X * Z)] = numer[pl.ds(pl.multiple_of(own_row, SHARD), SHARD), :]

    for where in others:
        sum_move(0, slot_of(*where), slot_of(*where), partner).wait_recv()
    sum_move(0, 0, (1 - y) * (X * Z), partner).wait_recv()

    parts = arrived[...].astype(jnp.float32)
    lane = lax.broadcasted_iota(jnp.int32, parts.shape, 2)

    def figure_of(first):
        inside = (lane >= first) & (lane < first + 3)
        return jnp.sum(jnp.where(inside, parts, 0.0), axis=2, keepdims=True)

    tops, dens = figure_of(TOP), figure_of(DENS)
    over = tops - jnp.max(tops, axis=0, keepdims=True)
    summed = jnp.sum(parts * jnp.exp2(over + over), axis=0)
    mass = summed[:, MASS : MASS + 1] + summed[:, MASS + 1 : MASS + 2]
    mass = mass + summed[:, MASS + 2 : MASS + 3]
    risk_ref[...] = summed[:, 0:CATEGORIES] / mass
    dens_top = jnp.max(dens, axis=0, keepdims=True)
    dens_sum = jnp.sum(jnp.exp2(dens - dens_top), axis=0)
    density = dens_top[0] / LOG2E + jnp.log(dens_sum) - math.log(total_e)
    density_ref[...] = jnp.broadcast_to(density, (SHARD, 128)).T[0:1, 0:SHARD]

    @pl.when(y == 0)
    def _():
        for copy in first_away:
            copy.wait_send()

    @pl.when(y == 1)
    def _():
        for copy in second_away:
            copy.wait_send()
        for name in FOUND_MOVES + HANDED_MOVES:
            move(name).wait_send()

    for name in EVERY_MOVES:
        move(name).wait_send()
    for k in range(1, groups):
        for n in range(chunks):
            hub_move(k, n).wait_send()
    for where in others:
        hand_out(*where).wait_send()
    hand_partner.wait_send()


def per_device(queries, exemplars, labels):
    groups = lax.axis_size("grp")
    devices = lax.axis_size("idx")
    local_q, depth = queries.shape
    local_e = exemplars.shape[0]
    group_q = local_q * devices
    f32, bf16 = jnp.float32, jnp.bfloat16
    vmem, dma = pltpu.VMEM, pltpu.SemaphoreType.DMA
    chunks = local_e // WIDE
    here = pl.BlockSpec(memory_space=pltpu.VMEM)
    away = pl.BlockSpec(memory_space=pl.ANY)
    risk, density = pl.pallas_call(
        functools.partial(kernel, groups, group_q * groups, local_e * devices),
        out_shape=(
            jax.ShapeDtypeStruct((local_q, CATEGORIES), f32),
            jax.ShapeDtypeStruct((1, local_q), f32),
        ),
        in_specs=[here, away, away],
        out_specs=(here, here),
        scratch_shapes=[
            vmem((group_q, depth), bf16),
            vmem((local_e, depth), bf16),
            vmem((CATEGORIES, local_e), jnp.int32),
            vmem((128, local_e), bf16),
            *[vmem((BLOCK, local_e), f32)] * 4,
            *[vmem((BLOCK, 128), f32)] * 2,
            *[vmem((group_q, 128), f32)] * 2,
            *[vmem((8, local_e), f32)] * 4,
            vmem((group_q, 128), f32),
            vmem((groups, local_e // 128, 128), f32),
            vmem((1, local_e), f32),
            vmem((group_q, 128), bf16),
            vmem((SENDERS, SHARD, 128), bf16),
            dma((chunks + 1,)),
            dma((N_MOVES,)),
            dma((N_MOVES,)),
            dma((2 * X - 1,)),
            dma((groups, chunks)),
            dma((groups, chunks)),
            dma((SENDERS,)),
            dma((SENDERS,)),
        ],
        compiler_params=pltpu.CompilerParams(
            collective_id=0, has_side_effects=True, vmem_limit_bytes=58 * 2**20
        ),
        cost_estimate=pl.CostEstimate(
            flops=2 * group_q * local_e * (depth + 128),
            bytes_accessed=local_e * depth * 2 + local_e * CATEGORIES * 4,
            transcendentals=3 * group_q * local_e,
        ),
        name="prefilter",
    )(queries, exemplars, labels.T)
    return risk, density.reshape(local_q)


def solution(mesh):
    in_specs = (P(("grp", "idx"), None), P("idx", None), P("idx", None))
    out_specs = (P(("grp", "idx"), None), P(("grp", "idx")))
    return jax.shard_map(
        per_device, mesh=mesh, in_specs=in_specs, out_specs=out_specs, check_vma=False
    )
```

time: 69.5 us -> 60.9 us (0.88)
  Pallas kernels: 66.2 us -> 57.6 us
    pallas_call x1, Pallas kernels: 66.2 us -> 57.6 us  [per_device(): pl.pallas_call(functools.partial(kernel, groups, group_q * groups, local_...]
where the time goes in v2:
time: 60.9 us; the launch traced here: 60.7 us
  Pallas kernels  57.6 us (95%)
  local copies, waits for them, and re-layouts  2.43 us (4%)
  between operations  0.64 us (1%)
    pallas_call x1, Pallas kernels, per_device(): pl.pallas_call(functools.partial(kernel, groups, group_q * groups, local_...  57.6 us
    unnamed x2, local copies, waits for them, and re-layouts  2.43 us

profile of v2, /device:TPU:1, one launch (start us, length us, event | category | flops | bytes accessed | tf_op | source)
XLA Modules:
  0.0 60.7 jit_solution(3445400098546683922)
XLA Ops:
  0.6 57.6 %prefilter.1 = (f32[16,64]{1,0:T(8,128)}, f32[1,16]{1,0:T(1,128)}) custom-call(bf16[16,1024]{1,0:T(8,128)(2,1)} %q_ref.1, bf16[4096,1024]{1,0:T(8,128)(2,1)} %ex_hbm.1, s32[64,4096]{1,0:T(8,128)} %bitcast.2), custom_call_target="tpu_custom_call" | custom-call | flops 9663676416 | bytes 9437184 | tf_op jit(solution)/shard_map/prefilter/pallas_call | solution.py:474
  58.2 1.3 %copy.7 = f32[16,64]{1,0:T(8,128)} copy(f32[16,64]{1,0:T(8,128)} %get-tuple-element.8) | data formatting | bytes 8192
  59.5 1.1 %copy.8 = f32[16]{0:T(128)} copy(f32[16]{0:T(128)} %bitcast.3) | data formatting | bytes 128

commit v3 on v2

--- a/solution.py
+++ b/solution.py
@@ -12,9 +12,6 @@
 SHARD = 16
 X_ORDER = (0, 1, -1, 2)
 Z_ORDER = (0, 1, -1, 2, -2, 3, -3, 4)
-FIRST_BASE = {0: 0, 1: 64, -1: 128, 2: 256, -2: 320, 3: 768, -3: 832, 4: 896}
-NEAR_BASE = {0: 192, 1: 384, -1: 448, 2: 704}
-FAR_BASE = {0: 512, 1: 576, -1: 640, 2: 960}
 PIECES = ((0, 1), (1, 2), (2, 1), (-2, 1), (3, 2), (4, 1))
 BLOCK = 256
 WIDE = 1024
@@ -25,23 +22,41 @@
 MESH = pl.DeviceIdType.MESH
 
 
+def lay_out():
+    def first(half, *dzs):
+        return [(0, dx, dz) for dz in dzs for dx in X_ORDER[2 * half : 2 * half + 2]]
+
+    order = first(0, 0) + first(1, 0) + first(0, 1, -1)
+    order += [(1, 0, 0), (1, 0, 1), (1, 0, -1), (1, 0, 2)]
+    order += [(1, 1, 0), (1, -1, 0), (1, -1, 1), (1, -1, -1)]
+    order += first(1, 1, -1)
+    order += [(1, 1, 1), (1, 1, -1), (1, 0, -2), (1, 1, 2), (1, -1, 2), (1, 1, -2), (1, -1, -2)]
+    order += [(1, 2, 0), (1, 0, 3), (1, 0, -3), (1, 2, 1), (1, 2, -1)]
+    order += first(0, 2, -2) + first(1, 2, -2)
+    order += [(1, 0, 4), (1, 2, 2), (1, 2, -2)]
+    order += [(1, 1, 3), (1, 1, -3), (1, -1, 3), (1, -1, -3), (1, 1, 4)]
+    order += first(0, 3, -3) + first(1, 3, -3) + first(0, 4) + first(1, 4)
+    order += [(1, -1, 4), (1, 2, 3), (1, 2, -3), (1, 2, 4)]
+    return {place: SHARD * i for i, place in enumerate(order)}
+
+
+ROW_OF = lay_out()
+
+
 def row_of(side, dx, dz):
-    if side == 0:
-        return FIRST_BASE[dz] + SHARD * X_ORDER.index(dx)
-    at = Z_ORDER.index(dz)
-    return NEAR_BASE[dx] + SHARD * at if at < 4 else FAR_BASE[dx] + SHARD * (at - 4)
+    return ROW_OF[side, dx, dz]
 
 
 def gather_moves():
     moves = {}
-    for k in (1, 2, 3, 4):
-        far = 4 if k == 4 else -k
-        for half in (0, 1):
-            off = 32 * half
-            if k < 4 or half == 0:
-                moves["z+", k, half] = (FIRST_BASE[1 - k] + off, 2, FIRST_BASE[far] + off, "zp")
-            if k < 4 or half == 1:
-                moves["z-", k, half] = (FIRST_BASE[k - 1] + off, 2, FIRST_BASE[k] + off, "zm")
+    moves["x2",] = (row_of(0, -1, 0), 1, row_of(0, 2, 0), "xp")
+    for half in (0, 1):
+        dx = X_ORDER[2 * half]
+        for k in (1, 2, 3):
+            moves["z+", k, half] = (row_of(0, dx, 1 - k), 2, row_of(0, dx, -k), "zp")
+            moves["z-", k, half] = (row_of(0, dx, k - 1), 2, row_of(0, dx, k), "zm")
+    moves["z+", 4, 0] = (row_of(0, X_ORDER[0], -2), 2, row_of(0, X_ORDER[0], 4), "zpp")
+    moves["z-", 4, 1] = (row_of(0, X_ORDER[2], 2), 2, row_of(0, X_ORDER[2], 4), "zmm")
     for g, (dz, count) in enumerate(PIECES):
         own = row_of(1, 0, dz)
         moves["v+", g] = (own, count, row_of(1, -1, dz), "xp")
@@ -53,16 +68,10 @@
     moves["w+", 3] = (row_of(1, 0, -2), 1, row_of(1, 0, -3), "zp")
     moves["w-", 3] = (row_of(1, 0, 2), 1, row_of(1, 0, 3), "zm")
     moves["w+", 4] = (row_of(1, 0, -2), 1, row_of(1, 0, 4), "zpp")
-    for g, (dz, count) in enumerate(PIECES):
-        if g > 0:
-            moves["f", g] = (row_of(1, 0, dz), count, row_of(1, 0, dz), "partner")
     return moves
 
 
 MOVES = gather_moves()
-EVERY_MOVES = [name for name in MOVES if name[0][0] in "zvu"]
-FOUND_MOVES = [name for name in MOVES if name[0] in ("w+", "w-")]
-HANDED_MOVES = [name for name in MOVES if name[0] == "f"]
 MOVE_IDS = {name: i for i, name in enumerate(MOVES)}
 FIRST_WAY = {(0, dx): len(MOVES) + i for i, dx in enumerate(X_ORDER)}
 SECOND_WAY = {dz: len(MOVES) + len(X_ORDER) + i for i, dz in enumerate(Z_ORDER[0:5])}
@@ -76,7 +85,7 @@
 
 def kernel(
     groups, total_q, total_e,
-    q_ref, ex_hbm, labels_hbm, risk_ref, density_ref,
+    q_ref, ex_hbm, labels_hbm, result_ref,
     rows, ex, labels_raw, labels, s0, s1, s2, s3,
     top_part0, top_part1, row_top, row_sum, peak0, peak1, col_max, col_sum,
     best, hubs, hub_row, numer, arrived,
@@ -98,9 +107,9 @@
 
     near = {
         "xp": place(1, 0, y), "xm": place(-1, 0, y), "zp": place(0, 1, y), "zm": place(0, -1, y),
-        "zpp": place(0, 2, y), "partner": place(0, 0, 1 - y),
+        "zpp": place(0, 2, y), "zmm": place(0, -2, y),
     }
-    partner = near["partner"]
+    partner = place(0, 0, 1 - y)
     peers = [(lax.rem(g + k, groups), me) for k in range(1, groups)]
 
     loads = [
@@ -117,7 +126,7 @@
     barrier = pltpu.get_barrier_semaphore()
     greeted = [partner, *peers]
     greeted += [place(dx, 0, side) for dx in X_ORDER[1:] for side in (0, 1)]
-    greeted += [place(0, dz, y) for dz in Z_ORDER[1:5]]
+    greeted += [place(0, dz, side) for dz in Z_ORDER[1:5] for side in (0, 1)]
     for other in greeted:
         pl.semaphore_signal(barrier, inc=1, device_id=other, device_id_type=MESH)
     pl.semaphore_wait(barrier, len(greeted))
@@ -147,22 +156,23 @@
         )
 
     first_away = [away(0, row_of(0, 0, 0), FIRST_WAY[0, 0], partner)]
-    for dx in X_ORDER[1:]:
-        back = dx if dx == 2 else -dx
+    for dx in X_ORDER[1:3]:
         for side in (0, 1):
             first_away.append(
-                away(
-                    len(first_away), row_of(0, back, 0), FIRST_WAY[0, back], place(dx, 0, side)
-                )
+                away(len(first_away), row_of(0, -dx, 0), FIRST_WAY[0, -dx], place(dx, 0, side))
             )
     second_away = [away(0, row_of(1, 0, 0), SECOND_WAY[0], partner)]
     for dz in Z_ORDER[1:5]:
-        second_away.append(
-            away(len(second_away), row_of(1, 0, -dz), SECOND_WAY[-dz], place(0, dz, y))
-        )
+        for side in (1, 0):
+            second_away.append(
+                away(len(second_away), row_of(1, 0, -dz), SECOND_WAY[-dz], place(0, dz, side))
+            )
 
     def landed(target, sem):
         away(0, target, sem, partner).wait_recv()
+
+    own_row = y * row_of(1, 0, 0)
+    rows[pl.ds(pl.multiple_of(own_row, SHARD), SHARD), :] = q_ref[...]
 
     @pl.when(y == 0)
     def _():
@@ -173,9 +183,7 @@
     def _():
         for copy in second_away:
             copy.start()
-
-    own_row = y * row_of(1, 0, 0)
-    rows[pl.ds(pl.multiple_of(own_row, SHARD), SHARD), :] = q_ref[...]
+        go(("v+", 0), ("v-", 0))
 
     label_load.wait()
     rest = lax.broadcasted_iota(jnp.int32, (128 - CATEGORIES, WIDE), 0) + CATEGORIES
@@ -190,79 +198,59 @@
     @pl.when(y == 0)
     def _():
         landed(row_of(1, 0, 0), SECOND_WAY[0])
-
-    go(("v+", 0), ("v-", 0))
+        go(("v+", 0), ("v-", 0))
 
     @pl.when(y == 1)
     def _():
         landed(row_of(0, 0, 0), FIRST_WAY[0, 0])
-        landed(row_of(1, 0, 1), SECOND_WAY[1])
-        landed(row_of(1, 0, -1), SECOND_WAY[-1])
-        go(("f", 1), ("v+", 1), ("v-", 1))
-        landed(row_of(1, 0, 2), SECOND_WAY[2])
-        go(("f", 2), ("w-", 3), ("v+", 2), ("v-", 2))
-        landed(row_of(1, 0, -2), SECOND_WAY[-2])
-        go(("f", 3), ("w+", 3), ("w+", 4), ("v+", 3), ("v-", 3))
-
-    for dx in X_ORDER[1:]:
-        landed(row_of(0, dx, 0), FIRST_WAY[0, dx])
-    go(("z+", 1, 0), ("z-", 1, 0), ("z+", 1, 1), ("z-", 1, 1))
-
-    @pl.when(y == 0)
-    def _():
-        for g in (1, 2, 3):
-            got(("f", g))
-            go(("v+", g), ("v-", g))
-
-    for half in (0, 1):
-        got(("z+", 1, half), ("z-", 1, half))
-        go(("z+", 2, half), ("z-", 2, half))
+
+    landed(row_of(0, 1, 0), FIRST_WAY[0, 1])
+    go(("z+", 1, 0), ("z-", 1, 0))
+    landed(row_of(0, -1, 0), FIRST_WAY[0, -1])
+    go(("x2",))
+    landed(row_of(1, 0, 1), SECOND_WAY[1])
+    landed(row_of(1, 0, -1), SECOND_WAY[-1])
+    go(("v+", 1), ("v-", 1))
+    got(("v+", 0), ("v-", 0))
+    go(("u+", 0))
+    got(("x2",))
+    go(("z+", 1, 1), ("z-", 1, 1))
+    landed(row_of(1, 0, 2), SECOND_WAY[2])
+    go(("w-", 3), ("v+", 2), ("v-", 2))
+    landed(row_of(1, 0, -2), SECOND_WAY[-2])
+    go(("w+", 3), ("w+", 4), ("v+", 3), ("v-", 3))
+    got(("v+", 1))
+    go(("u+", 1))
+    got(("z+", 1, 0), ("z-", 1, 0))
+    go(("z+", 2, 0), ("z-", 2, 0))
 
     def event(at):
-        if at == (0, 1):
-            got(("v+", 0), ("v-", 0))
-            go(("u+", 0))
-        if at == (0, 2):
-
-            @pl.when(y == 1)
-            def _():
-                got(("w+", 3), ("w-", 3))
-                go(("f", 4), ("v+", 4), ("v-", 4))
-                got(("w+", 4))
-                go(("f", 5), ("v+", 5), ("v-", 5))
-
         if at == (0, 3):
-            got(("v+", 1), ("v-", 1))
-            go(("u+", 1))
-            got(("v+", 2), ("v-", 2))
-            go(("u-", 2))
-            got(("v+", 3), ("v-", 3))
-            go(("u-", 3))
+            got(("w+", 3), ("w-", 3))
+            go(("v+", 4), ("v-", 4))
+            got(("v+", 2), ("v-", 2), ("v+", 3), ("v-", 3))
+            go(("u-", 2), ("u-", 3))
         if at == (1, 0):
-            for half in (0, 1):
-                got(("z+", 2, half), ("z-", 2, half))
-                go(("z+", 3, half), ("z-", 3, half))
+            got(("z+", 1, 1), ("z-", 1, 1))
+            go(("z+", 2, 1), ("z-", 2, 1))
+            got(("w+", 4))
+            go(("v+", 5), ("v-", 5))
+            got(("v-", 1), ("u+", 0), ("u+", 1))
         if at == (1, 1):
-
-            @pl.when(y == 0)
-            def _():
-                for g in (4, 5):
-                    got(("f", g))
-                    go(("v+", g), ("v-", g))
-
+            got(("z+", 2, 0), ("z-", 2, 0))
+            go(("z+", 4, 0), ("z+", 3, 0), ("z-", 3, 0))
         if at == (1, 3):
-            got(("z+", 3, 0), ("z-", 3, 0))
-            go(("z+", 4, 0))
-        if at == (2, 0):
-            got(("z+", 3, 1), ("z-", 3, 1))
-            go(("z-", 4, 1))
             got(("v+", 4), ("v-", 4))
             go(("u-", 4))
+        if at == (2, 0):
+            got(("z+", 2, 1), ("z-", 2, 1))
+            go(("z-", 4, 1), ("z+", 3, 1), ("z-", 3, 1))
             got(("v+", 5), ("v-", 5))
             go(("u+", 5))
-            got(("u+", 0), ("u+", 1), ("u-", 2))
+            got(("u-", 2), ("u-", 3))
         if at == (3, 0):
-            got(("z+", 4, 0), ("z-", 4, 1), ("u-", 3), ("u-", 4), ("u+", 5))
+            got(("z+", 3, 0), ("z-", 3, 0), ("z+", 3, 1), ("z-", 3, 1))
+            got(("z+", 4, 0), ("z-", 4, 1), ("u-", 4), ("u+", 5))
 
     def score(b, n):
         at = pl.ds(n * WIDE, WIDE)
@@ -432,11 +420,11 @@
     summed = jnp.sum(parts * jnp.exp2(over + over), axis=0)
     mass = summed[:, MASS : MASS + 1] + summed[:, MASS + 1 : MASS + 2]
     mass = mass + summed[:, MASS + 2 : MASS + 3]
-    risk_ref[...] = summed[:, 0:CATEGORIES] / mass
     dens_top = jnp.max(dens, axis=0, keepdims=True)
     dens_sum = jnp.sum(jnp.exp2(dens - dens_top), axis=0)
     density = dens_top[0] / LOG2E + jnp.log(dens_sum) - math.log(total_e)
-    density_ref[...] = jnp.broadcast_to(density, (SHARD, 128)).T[0:1, 0:SHARD]
+    result_lane = lax.broadcasted_iota(jnp.int32, (SHARD, 128), 1)
+    result_ref[...] = jnp.where(result_lane < CATEGORIES, summed / mass, density)
 
     @pl.when(y == 0)
     def _():
@@ -447,10 +435,8 @@
     def _():
         for copy in second_away:
             copy.wait_send()
-        for name in FOUND_MOVES + HANDED_MOVES:
-            move(name).wait_send()
-
-    for name in EVERY_MOVES:
+
+    for name in MOVES:
         move(name).wait_send()
     for k in range(1, groups):
         for n in range(chunks):
@@ -458,6 +444,11 @@
     for where in others:
         hand_out(*where).wait_send()
     hand_partner.wait_send()
+
+
+def split_kernel(result_ref, risk_ref, density_ref):
+    risk_ref[...] = result_ref[:, 0:CATEGORIES]
+    density_ref[...] = result_ref[...].T[CATEGORIES : CATEGORIES + 1, 0:SHARD]
 
 
 def per_device(queries, exemplars, labels):
@@ -471,14 +462,11 @@
     chunks = local_e // WIDE
     here = pl.BlockSpec(memory_space=pltpu.VMEM)
     away = pl.BlockSpec(memory_space=pl.ANY)
-    risk, density = pl.pallas_call(
+    result = pl.pallas_call(
         functools.partial(kernel, groups, group_q * groups, local_e * devices),
-        out_shape=(
-            jax.ShapeDtypeStruct((local_q, CATEGORIES), f32),
-            jax.ShapeDtypeStruct((1, local_q), f32),
-        ),
+        out_shape=jax.ShapeDtypeStruct((local_q, 128), f32),
         in_specs=[here, away, away],
-        out_specs=(here, here),
+        out_specs=here,
         scratch_shapes=[
             vmem((group_q, depth), bf16),
             vmem((local_e, depth), bf16),
@@ -496,7 +484,7 @@
             dma((chunks + 1,)),
             dma((N_MOVES,)),
             dma((N_MOVES,)),
-            dma((2 * X - 1,)),
+            dma((9,)),
             dma((groups, chunks)),
             dma((groups, chunks)),
             dma((SENDERS,)),
@@ -512,6 +500,16 @@
         ),
         name="prefilter",
     )(queries, exemplars, labels.T)
+    risk, density = pl.pallas_call(
+        split_kernel,
+        out_shape=(
+            jax.ShapeDtypeStruct((local_q, CATEGORIES), f32),
+            jax.ShapeDtypeStruct((1, local_q), f32),
+        ),
+        in_specs=[here],
+        out_specs=(here, here),
+        name="split",
+    )(result)
     return risk, density.reshape(local_q)
 
 

time: 60.9 us -> 58.5 us (0.961)
  local copies, waits for them, and re-layouts: 2.43 us -> 0 us
    unnamed x2 -> x0, local copies, waits for them, and re-layouts: 2.43 us -> none
    pallas_call x0 -> x1, Pallas kernels: none -> 1.3 us  [per_device(): pl.pallas_call(split_kernel, out_shape=(jax.ShapeDtypeStruct((local_q, CA...]
    pallas_call x1, Pallas kernels: 57.6 us -> 56.4 us  [per_device(): pl.pallas_call(functools.partial(kernel, groups, group_q * groups, local_...]
where the time goes in v3:
time: 58.5 us; the launch traced here: 58.3 us
  Pallas kernels  57.7 us (99%)
  between operations  0.64 us (1%)
    pallas_call x1, Pallas kernels, per_device(): pl.pallas_call(functools.partial(kernel, groups, group_q * groups, local_...  56.4 us
    pallas_call x1, Pallas kernels, per_device(): pl.pallas_call(split_kernel, out_shape=(jax.ShapeDtypeStruct((local_q, CA...  1.3 us

profile of v3, /device:TPU:1, one launch (start us, length us, event | category | flops | bytes accessed | tf_op | source)
XLA Modules:
  0.0 58.3 jit_solution(17799709189037050509)
XLA Ops:
  0.6 56.4 %prefilter.1.result_ref = f32[16,128]{1,0:T(8,128)} custom-call(bf16[16,1024]{1,0:T(8,128)(2,1)} %q_ref.1, bf16[4096,1024]{1,0:T(8,128)(2,1)} %ex_hbm.1, s32[64,4096]{1,0:T(8,128)} %bitcast.2), custom_call_target="tpu_custom_call" | custom-call | flops 9663676416 | bytes 9437184 | tf_op jit(solution)/shard_map/prefilter/pallas_call | solution.py:465
  57.0 1.3 %split.1 = (f32[16,64]{1,0:T(8,128)}, f32[1,16]{1,0:T(1,128)}) custom-call(f32[16,128]{1,0:T(8,128)} %prefilter.1.result_ref), custom_call_target="tpu_custom_call" | custom-call | tf_op jit(solution)/shard_map/split/pallas_call | solution.py:503

commit v4 on v3

--- a/solution.py
+++ b/solution.py
@@ -309,12 +309,15 @@
     blocks = len(scores)
     final = blocks - 1
     for b in range(blocks):
+        if b == final:
+            for n in range(chunks):
+                total(b - 1, n)
         for n in range(chunks):
             event((b, n))
             if b == 0:
                 loads[n].wait()
             score(b, n)
-            if b > 0:
+            if 0 < b < final:
                 total(b - 1, n)
             if b == final:
                 total(b, n, rowwise=False)
@@ -404,25 +407,45 @@
     hand_partner.start()
     arrived[y * (X * Z)] = numer[pl.ds(pl.multiple_of(own_row, SHARD), SHARD), :]
 
-    for where in others:
-        sum_move(0, slot_of(*where), slot_of(*where), partner).wait_recv()
+    lane = lax.broadcasted_iota(jnp.int32, (SHARD, 128), 1)
+    in_top = (lane >= TOP) & (lane < DENS)
+    in_dens = (lane >= DENS) & (lane < UNUSED)
+
+    def join(slots):
+        parts = [arrived[slot].astype(jnp.float32) for slot in slots]
+        tops = [jnp.sum(jnp.where(in_top, p, 0.0), axis=1, keepdims=True) for p in parts]
+        dens = [jnp.sum(jnp.where(in_dens, p, 0.0), axis=1, keepdims=True) for p in parts]
+        top = functools.reduce(jnp.maximum, tops)
+        dens_top = functools.reduce(jnp.maximum, dens)
+        summed = jnp.zeros((SHARD, 128), jnp.float32)
+        dens_sum = jnp.zeros((SHARD, 1), jnp.float32)
+        for part, mine, own_dens in zip(parts, tops, dens):
+            summed = summed + part * jnp.exp2(2.0 * (mine - top))
+            dens_sum = dens_sum + jnp.exp2(own_dens - dens_top)
+        return top, summed, dens_top, dens_sum
+
+    late = {
+        (dx, dz)
+        for side, dx, dz in ROW_OF
+        if row_of(side, dx, dz) < BLOCK
+    }
+    early_slots = [slot_of(*where) for where in others if where[1:] not in late]
+    late_slots = [slot_of(*where) for where in others if where[1:] in late]
+    for slot in early_slots:
+        sum_move(0, slot, slot, partner).wait_recv()
+    top_a, summed_a, dens_top_a, dens_sum_a = join(early_slots)
+    for slot in late_slots:
+        sum_move(0, slot, slot, partner).wait_recv()
     sum_move(0, 0, (1 - y) * (X * Z), partner).wait_recv()
-
-    parts = arrived[...].astype(jnp.float32)
-    lane = lax.broadcasted_iota(jnp.int32, parts.shape, 2)
-
-    def figure_of(first):
-        inside = (lane >= first) & (lane < first + 3)
-        return jnp.sum(jnp.where(inside, parts, 0.0), axis=2, keepdims=True)
-
-    tops, dens = figure_of(TOP), figure_of(DENS)
-    over = tops - jnp.max(tops, axis=0, keepdims=True)
-    summed = jnp.sum(parts * jnp.exp2(over + over), axis=0)
+    top_b, summed_b, dens_top_b, dens_sum_b = join([*late_slots, 0, X * Z])
+    top = jnp.maximum(top_a, top_b)
+    summed = summed_a * jnp.exp2(2.0 * (top_a - top)) + summed_b * jnp.exp2(2.0 * (top_b - top))
     mass = summed[:, MASS : MASS + 1] + summed[:, MASS + 1 : MASS + 2]
     mass = mass + summed[:, MASS + 2 : MASS + 3]
-    dens_top = jnp.max(dens, axis=0, keepdims=True)
-    dens_sum = jnp.sum(jnp.exp2(dens - dens_top), axis=0)
-    density = dens_top[0] / LOG2E + jnp.log(dens_sum) - math.log(total_e)
+    dens_top = jnp.maximum(dens_top_a, dens_top_b)
+    dens_sum = dens_sum_a * jnp.exp2(dens_top_a - dens_top)
+    dens_sum = dens_sum + dens_sum_b * jnp.exp2(dens_top_b - dens_top)
+    density = dens_top / LOG2E + jnp.log(dens_sum) - math.log(total_e)
     result_lane = lax.broadcasted_iota(jnp.int32, (SHARD, 128), 1)
     result_ref[...] = jnp.where(result_lane < CATEGORIES, summed / mass, density)
 

time: 58.5 us -> 57.7 us (0.986)
  Pallas kernels: 57.7 us -> 56.9 us
    pallas_call x1, Pallas kernels: 56.4 us -> 55.6 us  [per_device(): pl.pallas_call(functools.partial(kernel, groups, group_q * groups, local_...]
where the time goes in v4:
time: 57.7 us; the launch traced here: 57.5 us
  Pallas kernels  56.9 us (99%)
  between operations  0.64 us (1%)
    pallas_call x1, Pallas kernels, per_device(): pl.pallas_call(functools.partial(kernel, groups, group_q * groups, local_...  55.6 us
    pallas_call x1, Pallas kernels, per_device(): pl.pallas_call(split_kernel, out_shape=(jax.ShapeDtypeStruct((local_q, CA...  1.3 us

profile of v4, /device:TPU:1, one launch (start us, length us, event | category | flops | bytes accessed | tf_op | source)
XLA Modules:
  0.0 57.5 jit_solution(14517369340377549429)
XLA Ops:
  0.6 55.6 %prefilter.1.result_ref = f32[16,128]{1,0:T(8,128)} custom-call(bf16[16,1024]{1,0:T(8,128)(2,1)} %q_ref.1, bf16[4096,1024]{1,0:T(8,128)(2,1)} %ex_hbm.1, s32[64,4096]{1,0:T(8,128)} %bitcast.2), custom_call_target="tpu_custom_call" | custom-call | flops 9663676416 | bytes 9437184 | tf_op jit(solution)/shard_map/prefilter/pallas_call | solution.py:488
  56.2 1.3 %split.1 = (f32[16,64]{1,0:T(8,128)}, f32[1,16]{1,0:T(1,128)}) custom-call(f32[16,128]{1,0:T(8,128)} %prefilter.1.result_ref), custom_call_target="tpu_custom_call" | custom-call | tf_op jit(solution)/shard_map/split/pallas_call | solution.py:526

commit v5 on v4

--- a/solution.py
+++ b/solution.py
@@ -125,7 +125,7 @@
 
     barrier = pltpu.get_barrier_semaphore()
     greeted = [partner, *peers]
-    greeted += [place(dx, 0, side) for dx in X_ORDER[1:] for side in (0, 1)]
+    greeted += [place(dx, 0, side) for dx in X_ORDER[1:3] for side in (0, 1)]
     greeted += [place(0, dz, side) for dz in Z_ORDER[1:5] for side in (0, 1)]
     for other in greeted:
         pl.semaphore_signal(barrier, inc=1, device_id=other, device_id_type=MESH)

time: 57.7 us -> 57.7 us (level)
  no operation moved by 1% of the time
where the time goes in v5:
time: 57.7 us; the launch traced here: 57.5 us
  Pallas kernels  56.8 us (98%)
  between operations  0.64 us (1%)
    pallas_call x1, Pallas kernels, per_device(): pl.pallas_call(functools.partial(kernel, groups, group_q * groups, local_...  55.5 us
    pallas_call x1, Pallas kernels, per_device(): pl.pallas_call(split_kernel, out_shape=(jax.ShapeDtypeStruct((local_q, CA...  1.3 us

profile of v5, /device:TPU:1, one launch (start us, length us, event | category | flops | bytes accessed | tf_op | source)
XLA Modules:
  0.0 57.5 jit_solution(13211543049830621080)
XLA Ops:
  0.6 55.5 %prefilter.1.result_ref = f32[16,128]{1,0:T(8,128)} custom-call(bf16[16,1024]{1,0:T(8,128)(2,1)} %q_ref.1, bf16[4096,1024]{1,0:T(8,128)(2,1)} %ex_hbm.1, s32[64,4096]{1,0:T(8,128)} %bitcast.2), custom_call_target="tpu_custom_call" | custom-call | flops 9663676416 | bytes 9437184 | tf_op jit(solution)/shard_map/prefilter/pallas_call | solution.py:488
  56.2 1.3 %split.1 = (f32[16,64]{1,0:T(8,128)}, f32[1,16]{1,0:T(1,128)}) custom-call(f32[16,128]{1,0:T(8,128)} %prefilter.1.result_ref), custom_call_target="tpu_custom_call" | custom-call | tf_op jit(solution)/shard_map/split/pallas_call | solution.py:526
